TPU v7x, 256 devices: a whole 4x4x8 slice. The times are simulated.
256 devices in a mesh: quad: 16 (over z_lo, x), sx: 4 (over z_hi, core), sy: 4 (over y).
Axes of the slice: x: 4, y: 4, z: 8 (z_hi: 2, z_lo: 4; z = z_hi * 4 + z_lo), core: 2. Of those that a mesh axis runs over, the one named last changes fastest.
Arguments:
- probes: bfloat16 [64, 64, 32, 128], P(None, 'sx', 'sy'), may hold values from -6 to 6
- quad_index: int32 [16], P('quad'), may hold values from 0 to 63
- region_label: int32 [64, 64, 32], replicated, may hold values from 0 to 7
- gain_label: int32 [64, 64, 32], replicated, may hold values from 0 to 7
- region_eps: float32 [8], replicated, may hold values from 1 to 3
- gain_rate: float32 [8], replicated, may hold values from 1 to 8
Outputs:
- moment0: float32 [64, 64, 32, 128], P('quad', 'sx', 'sy')
- moment1: float32 [64, 64, 32, 128], P('quad', 'sx', 'sy')
- projections: float32 [2, 2, 64, 64], replicated
All inputs are finite; a program needn't handle non-finite values.
Results may differ from a plain program's by a relative error of at most 0.0003.
Values may be sent and summed in bfloat16 or wider, within the bound.
No kernel may reach another device: no remote copies, remote signals or barrier semaphores. Data moves between devices by JAX's collectives and lax.ppermute only.
A program may use at most 128 MiB of HBM per device.

v0:
```python
import math
import jax
import jax.numpy as jnp
from jax import lax
from jax.sharding import PartitionSpec as P

QUAD = 16


def with_halo(block, sides, width):
    for axis, dim in sides:
        count = lax.axis_size(axis)
        forward = [(i, i + 1) for i in range(count - 1)]
        backward = [(target, source) for source, target in forward]
        low = lax.ppermute(
            lax.slice_in_dim(block, block.shape[dim] - width, None, axis=dim), axis, forward
        )
        high = lax.ppermute(lax.slice_in_dim(block, 0, width, axis=dim), axis, backward)
        block = jnp.concatenate([low, block, high], axis=dim)
    return block


def multiply_by(coef_real, coef_imag, field):
    half = field.shape[-1] // 2
    field_real = field[..., :half]
    field_imag = field[..., half:]
    return jnp.concatenate(
        [
            coef_real * field_real - coef_imag * field_imag,
            coef_real * field_imag + coef_imag * field_real,
        ],
        axis=-1,
    )


def plane_sum(padded):
    total = padded[:, :, 2:, 1:-1] + padded[:, :, :-2, 1:-1]
    return total + padded[:, :, 1:-1, 2:] + padded[:, :, 1:-1, :-2]


def depth_sum(field):
    padded = jnp.pad(field, ((0, 0), (1, 1), (0, 0), (0, 0), (0, 0)))
    return padded[:, 2:] + padded[:, :-2]


def lookup(table, labels):
    levels = jnp.arange(table.shape[0], dtype=jnp.int32)
    return jnp.sum(jnp.where(labels[..., None] == levels, table, 0.0), axis=-1)[..., None]


def inverse_of(mat_real, mat_imag, node_real, node_imag):
    diag_real = 6.0 + node_real * mat_real - node_imag * mat_imag
    diag_imag = node_real * mat_imag + node_imag * mat_real
    modulus = diag_real * diag_real + diag_imag * diag_imag
    return (diag_real / modulus, -diag_imag / modulus)


def assemble(cross, half):
    blocks = []
    for moment in range(2):
        first_col = 2 * half * moment
        real_cols = cross[:, first_col : first_col + half]
        imag_cols = cross[:, first_col + half : first_col + 2 * half]
        blocks.append(
            jnp.stack([real_cols[:half] + imag_cols[half:], imag_cols[:half] - real_cols[half:]])
        )
    return jnp.stack(blocks)


def local_cross(left, right):
    columns = left.shape[-1]
    return lax.dot_general(
        left.reshape(-1, columns),
        right.reshape(-1, 2 * columns),
        (((0,), (0,)), ((), ())),
        precision=lax.Precision.HIGHEST,
        preferred_element_type=jnp.float32,
    )


def body(probes, quad_index, region_label, gain_label, region_eps, gain_rate):
    depth_cells, cells_x, cells_y, columns = probes.shape
    start_x = lax.axis_index("sx") * cells_x
    start_y = lax.axis_index("sy") * cells_y
    angle_node = 2.0 * math.pi * (quad_index.astype(jnp.float32) + 0.5) / (4 * QUAD)
    angle_node = angle_node[:, None, None, None, None]
    weight_real = jnp.cos(angle_node)
    weight_imag = jnp.sin(angle_node)
    node_real = 2.0 + weight_real
    source = probes.astype(jnp.float32)[None]
    region_block = lax.dynamic_slice(
        region_label, (0, start_x, start_y), (depth_cells, cells_x, cells_y)
    )
    gain_block = lax.dynamic_slice(
        gain_label, (0, start_x, start_y), (depth_cells, cells_x, cells_y)
    )
    inverse_real, inverse_imag = inverse_of(
        lookup(region_eps, region_block), lookup(gain_rate, gain_block), node_real, weight_imag
    )
    iterate = multiply_by(inverse_real, inverse_imag, source)
    for sweep in range(2):
        padded = with_halo(iterate, (("sx", 2), ("sy", 3)), 1)
        iterate = multiply_by(
            inverse_real, inverse_imag, source + plane_sum(padded) + depth_sum(iterate)
        )
    scaled_real = weight_real * node_real - weight_imag * weight_imag
    scaled_imag = weight_real * weight_imag + weight_imag * node_real
    first = jnp.sum(multiply_by(weight_real, weight_imag, iterate), axis=0)
    second = jnp.sum(multiply_by(scaled_real, scaled_imag, iterate), axis=0)
    both = jnp.concatenate([first, second], axis=-1)
    reduced = lax.psum_scatter(both, "quad", scatter_dimension=0, tiled=True)
    slab_rows = reduced.shape[0]
    start_z = lax.axis_index("quad") * slab_rows
    slab_source = lax.dynamic_slice_in_dim(probes, start_z, slab_rows, 0).astype(jnp.float32)
    summed = lax.psum(local_cross(slab_source, reduced), ("quad", "sx", "sy"))
    cells_total = depth_cells * cells_x * cells_y * lax.axis_size("sx") * lax.axis_size("sy")
    projections = assemble(summed, columns // 2) / cells_total
    return (reduced[..., :columns], reduced[..., columns:], projections)


def solution(mesh):
    placed = (P(None, "sx", "sy", None), P("quad"), P(), P(), P(), P())
    return jax.shard_map(
        body,
        mesh=mesh,
        in_specs=placed,
        out_specs=(P("quad", "sx", "sy", None), P("quad", "sx", "sy", None), P()),
        check_vma=False,
    )
```

profile of v0, /device:TPU:8, one launch (start us, length us, event | category | flops | bytes accessed | tf_op | source)
XLA Modules:
  0.0 496.3 jit_solution(4955377792394716702)
XLA Ops:
  14.9 3.8 multiply_add_fusion.4
  20.2 3.0 collective-permute-start.1
  24.4 2.4 pad_maximum_fusion.34
  26.8 4.1 collective-permute-start.2
  30.9 1.9 collective-permute-start.3
  32.9 3.1 pad_maximum_fusion.25
  36.0 2.7 collective-permute-done.2
  38.7 4.1 collective-permute-done.3
  42.8 13.2 %fusion.7 = f32[1,64,16,8,128]{4,3,2,1,0:T(8,128)} fusion(f32[1,64,18,1,128]{4,3,2,1,0:T(1,128)} %collective-permute-done.3, f32[1,64,1,8,128]{4,3,2,1,0:T(8,128)S(1)} %collective-permute-done, f32[1,64,1,8,128]{4,3,2,1,0:T(8,128)} %copy-done.6, f32[1,64,16,8,64]{4,3,2,1,0:T(8,128)S(1)} %get-tuple-element.19, f32[1,64,16,8,64]{4,3,2,1,0:T(8,128)} %copy-done.1, ...), kind=kLoop, calls=%fused_computation.21 | loop fusion | flops 19922944 | bytes 16384000 | tf_op jit(solution)/shard_map/add | solution.py:104
  56.0 7.1 %multiply_add_fusion.3 = (f32[1,64,16,8,64]{4,3,2,1,0:T(8,128)S(1)}, f32[1,64,16,8,64]{4,3,2,1,0:T(8,128)S(1)}) fusion(f32[1,64,16,8,128]{4,3,2,1,0:T(8,128)} %fusion.7, f32[64,16,8]{2,1,0:T(8,128)} %copy.16, f32[64,16,8]{2,1,0:T(8,128)} %copy.15), kind=kLoop, calls=%fused_computation.43 | loop fusion | flops 3145728 | bytes 8454144 | tf_op jit(solution)/shard_map/add | solution.py:30
  64.6 10.2 %collective-permute-start.5 = (f32[1,64,1,8,128]{4,3,2,1,0:T(8,128)S(1)}, f32[1,64,1,8,128]{4,3,2,1,0:T(8,128)S(1)}, u32[]{:S(2)}, u32[]{:S(2)}) collective-permute-start(f32[1,64,1,8,128]{4,3,2,1,0:T(8,128)S(1)} %get-tuple-element.13), channel_id=1, source_target_pairs={{0,4},{4,8},{8,12},{1,5},{5,9},{9,13},{2,6},{6,10},{10,14},{3,7},{... | collective-permute-start | bytes 786440 | tf_op jit(solution)/shard_map/ppermute | solution.py:15
  75.9 2.4 pad_maximum_fusion.30
  78.3 1.9 collective-permute-start.6
  80.3 4.1 collective-permute-start.7
  84.4 3.1 pad_maximum_fusion.26
  87.5 2.7 collective-permute-done.6
  90.2 1.9 collective-permute-done.7
  92.1 13.2 %fusion.2 = f32[1,64,16,8,128]{4,3,2,1,0:T(8,128)} fusion(f32[1,64,18,1,128]{4,3,2,1,0:T(1,128)} %collective-permute-done.7, f32[1,64,1,8,128]{4,3,2,1,0:T(8,128)S(1)} %collective-permute-done.4, f32[1,64,1,8,128]{4,3,2,1,0:T(8,128)} %copy-done.5, f32[1,64,16,8,64]{4,3,2,1,0:T(8,128)S(1)} %get-tuple-element.17, f32[1,64,16,8,64]{4,3,2,1,0:T(8,128)} %copy-done, ...), kind=kLoop, calls=%fused_computation.4 | loop fusion | flops 19922944 | bytes 16384000 | tf_op jit(solution)/shard_map/add | solution.py:104
  105.4 6.9 %multiply_subtract_fusion.1 = (f32[1,64,16,8,64]{4,3,2,1,0:T(8,128)S(1)}, f32[1,64,16,8,64]{4,3,2,1,0:T(8,128)S(1)}, f32[1,64,16,8,64]{4,3,2,1,0:T(8,128)S(1)}) fusion(f32[]{:T(128)} %bitcast.3, f32[]{:T(128)} %bitcast, f32[1,64,16,8,128]{4,3,2,1,0:T(8,128)} %fusion.2, f32[64,16,8]{2,1,0:T(8,128)} %copy.16, f32[64,16,8]{2,1,0:T(8,128)} %copy.15), kind=kLoop, calls=%fused_computation.40 | loop fusion | flops 4718592 | bytes 10551304 | tf_op jit(solution)/shard_map/sub | solution.py:29
  112.3 2.4 multiply_add_fusion.1
  117.0 4.0 pad_maximum_fusion
  121.1 121.8 %reduce-scatter.2.cloned.1.call-done = f32[4,16,8,256]{3,2,1,0:T(8,128)} async-done(((f32[64,16,8,256]{3,2,1,0:T(8,128)}), f32[4,16,8,256]{3,2,1,0:T(8,128)}) %reduce-scatter.2.cloned.1.call-update) | async-done | bytes 524304 | tf_op jit(solution)/shard_map/reduce_scatter | solution.py:111
  242.8 2.2 convolution_bitcast_fusion
  246.9 240.9 %all-reduce.4.cloned.1.call-done = f32[128,256]{1,0:T(8,128)} async-done(((f32[128,256]{1,0:T(8,128)}), f32[128,256]{1,0:T(8,128)}) %all-reduce.4.cloned.1.call-update) | async-done | bytes 131088 | tf_op jit(solution)/shard_map/psum | solution.py:115
  (43 shorter events, 17.8 us)
Async XLA Ops:
  7.2 6.5 %copy-start.2 = (bf16[64,16,8,128]{3,2,1,0:T(8,128)(2,1)S(1)}, bf16[64,16,8,128]{3,2,1,0:T(8,128)(2,1)}, u32[]{:S(2)}) copy-start(bf16[64,16,8,128]{3,2,1,0:T(8,128)(2,1)} %param.6) | copy-start | bytes 6291460
  7.2 235.7 %reduce-scatter.2.cloned.1.call-start = ((), (), s32[]{:S(2)}) async-start(), calls=%async_computation.1 | async-start | bytes 8912896 | tf_op jit(solution)/shard_map/reduce_scatter | solution.py:111
  13.7 1.0 copy-start.3
  13.7 1.2 copy-start.4
  18.7 14.1 %copy-start.1 = (f32[1,64,16,8,64]{4,3,2,1,0:T(8,128)}, f32[1,64,16,8,64]{4,3,2,1,0:T(8,128)S(1)}, u32[]{:S(2)}) copy-start(f32[1,64,16,8,64]{4,3,2,1,0:T(8,128)S(1)} %get-tuple-element.20) | copy-start | bytes 6291460
  18.9 4.4 collective-permute-start
  20.2 4.2 collective-permute-start.1
  24.4 2.4 copy-start.6
  26.8 11.9 %collective-permute-start.2 = (f32[1,64,18,1,128]{4,3,2,1,0:T(1,128)S(1)}, f32[1,64,18,1,128]{4,3,2,1,0:T(1,128)}, u32[]{:S(2)}, u32[]{:S(2)}) collective-permute-start(f32[1,64,18,1,128]{4,3,2,1,0:T(1,128)S(1)} %get-tuple-element.8), channel_id=1, source_target_pairs={{1,0},{2,1},{3,2},{5,4},{6,5},{7,6},{9,8},{10,9},{11,10},{13,12},{... | collective-permute-start | bytes 1769480 | tf_op jit(solution)/shard_map/ppermute | solution.py:18
  30.9 11.9 %collective-permute-start.3 = (f32[1,64,18,1,128]{4,3,2,1,0:T(1,128)S(1)}, f32[1,64,18,1,128]{4,3,2,1,0:T(1,128)}, u32[]{:S(2)}, u32[]{:S(2)}) collective-permute-start(f32[1,64,18,1,128]{4,3,2,1,0:T(1,128)S(1)} %get-tuple-element.9), channel_id=1, source_target_pairs={{0,1},{1,2},{2,3},{4,5},{5,6},{6,7},{8,9},{9,10},{10,11},{12,13},{... | collective-permute-start | bytes 1769480 | tf_op jit(solution)/shard_map/ppermute | solution.py:15
  63.1 21.3 %copy-start = (f32[1,64,16,8,64]{4,3,2,1,0:T(8,128)}, f32[1,64,16,8,64]{4,3,2,1,0:T(8,128)S(1)}, u32[]{:S(2)}) copy-start(f32[1,64,16,8,64]{4,3,2,1,0:T(8,128)S(1)} %get-tuple-element.18) | copy-start | bytes 6291460
  63.3 11.5 %collective-permute-start.4 = (f32[1,64,1,8,128]{4,3,2,1,0:T(8,128)S(1)}, f32[1,64,1,8,128]{4,3,2,1,0:T(8,128)S(1)}, u32[]{:S(2)}, u32[]{:S(2)}) collective-permute-start(f32[1,64,1,8,128]{4,3,2,1,0:T(8,128)S(1)} %get-tuple-element.14), channel_id=1, source_target_pairs={{4,0},{8,4},{12,8},{5,1},{9,5},{13,9},{6,2},{10,6},{14,10},{7,3},{... | collective-permute-start | bytes 786440 | tf_op jit(solution)/shard_map/ppermute | solution.py:18
  64.6 11.3 %collective-permute-start.5 = (f32[1,64,1,8,128]{4,3,2,1,0:T(8,128)S(1)}, f32[1,64,1,8,128]{4,3,2,1,0:T(8,128)S(1)}, u32[]{:S(2)}, u32[]{:S(2)}) collective-permute-start(f32[1,64,1,8,128]{4,3,2,1,0:T(8,128)S(1)} %get-tuple-element.13), channel_id=1, source_target_pairs={{0,4},{4,8},{8,12},{1,5},{5,9},{9,13},{2,6},{6,10},{10,14},{3,7},{... | collective-permute-start | bytes 786440 | tf_op jit(solution)/shard_map/ppermute | solution.py:15
  75.9 2.4 copy-start.5
  78.3 11.9 %collective-permute-start.6 = (f32[1,64,18,1,128]{4,3,2,1,0:T(1,128)S(1)}, f32[1,64,18,1,128]{4,3,2,1,0:T(1,128)}, u32[]{:S(2)}, u32[]{:S(2)}) collective-permute-start(f32[1,64,18,1,128]{4,3,2,1,0:T(1,128)S(1)} %get-tuple-element.6), channel_id=1, source_target_pairs={{1,0},{2,1},{3,2},{5,4},{6,5},{7,6},{9,8},{10,9},{11,10},{13,12},{... | collective-permute-start | bytes 1769480 | tf_op jit(solution)/shard_map/ppermute | solution.py:18
  80.3 11.9 %collective-permute-start.7 = (f32[1,64,18,1,128]{4,3,2,1,0:T(1,128)S(1)}, f32[1,64,18,1,128]{4,3,2,1,0:T(1,128)}, u32[]{:S(2)}, u32[]{:S(2)}) collective-permute-start(f32[1,64,18,1,128]{4,3,2,1,0:T(1,128)S(1)} %get-tuple-element.7), channel_id=1, source_target_pairs={{0,1},{1,2},{2,3},{4,5},{5,6},{6,7},{8,9},{9,10},{10,11},{12,13},{... | collective-permute-start | bytes 1769480 | tf_op jit(solution)/shard_map/ppermute | solution.py:15
  121.0 366.8 %all-reduce.4.cloned.1.call-start = ((), (), s32[]{:S(2)}) async-start(), calls=%async_computation.2 | async-start | bytes 262144 | tf_op jit(solution)/shard_map/psum | solution.py:115
Sparse Core Ops, SparseCore 0:
  121.1 121.6 reduce-scatter.1
  248.9 238.8 all-reduce.3
where the time goes:
time: 497 us; the launch traced here: 496 us
  waiting for transfers between devices  376 us (76%)
  other arithmetic  68.4 us (14%)
  starting transfers between devices  27.9 us (6%)
  between operations  15.3 us (3%)
  local copies, waits for them, and re-layouts  6.18 us (1%)
    psum x1, waiting for transfers between devices, body(): summed = lax.psum(local_cross(slab_source, reduced), ('quad', 'sx', 'sy'))  241 us
    reduce_scatter x1, waiting for transfers between devices, body(): reduced = lax.psum_scatter(both, 'quad', scatter_dimension=0, tiled=True)  122 us
    add x2, other arithmetic, body(): source + plane_sum(padded) + depth_sum(iterate)  26.4 us
    ppermute x4, starting transfers between devices, with_halo(): lax.ppermute(lax.slice_in_dim(block, block.shape[dim] - width, None, axis...  19.2 us
    add x3, other arithmetic, multiply_by(): coef_real * field_imag + coef_imag * field_real  13.3 us
  transfers between devices with their start and end apart: 10, of which 8 were waited for; matrix products, arithmetic and copies ran while one was open for 2% of the time, Pallas kernels for 0%

commit v1 on v0

--- a/solution.py
+++ b/solution.py
@@ -112,7 +112,7 @@
     slab_rows = reduced.shape[0]
     start_z = lax.axis_index("quad") * slab_rows
     slab_source = lax.dynamic_slice_in_dim(probes, start_z, slab_rows, 0).astype(jnp.float32)
-    summed = lax.psum(local_cross(slab_source, reduced), ("quad", "sx", "sy"))
+    summed = lax.psum(lax.psum(local_cross(slab_source, reduced), ("sx", "sy")), "quad")
     cells_total = depth_cells * cells_x * cells_y * lax.axis_size("sx") * lax.axis_size("sy")
     projections = assemble(summed, columns // 2) / cells_total
     return (reduced[..., :columns], reduced[..., columns:], projections)

time: 497 us -> 590 us (1.19)
  waiting for transfers between devices: 376 us -> 470 us
    psum x1 -> x2, waiting for transfers between devices: 241 us -> 335 us  [the longest x1 174 us: body(): lax.psum(local_cross(slab_source, reduced), ('sx', 'sy'))]
  transfers between devices with their start and end apart: 10 -> 11, of which waited for: 8 -> 9; matrix products, arithmetic and copies ran while one was open for 2% -> 1% of each run, Pallas kernels for 0% -> 0%
where the time goes in v1:
time: 590 us
  waiting for transfers between devices  470 us (80%)
  other arithmetic  68.4 us (12%)
  starting transfers between devices  28 us (5%)
  between operations  15 us (3%)
  local copies, waits for them, and re-layouts  6.18 us (1%)
    psum x1, waiting for transfers between devices, body(): lax.psum(local_cross(slab_source, reduced), ('sx', 'sy'))  174 us
    psum x1, waiting for transfers between devices, body(): lax.psum(lax.psum(local_cross(slab_source, reduced), ('sx', 'sy')), 'quad')  160 us
    reduce_scatter x1, waiting for transfers between devices, body(): reduced = lax.psum_scatter(both, 'quad', scatter_dimension=0, tiled=True)  122 us
    add x2, other arithmetic, body(): source + plane_sum(padded) + depth_sum(iterate)  26.4 us
    ppermute x4, starting transfers between devices, with_halo(): lax.ppermute(lax.slice_in_dim(block, block.shape[dim] - width, None, axis...  19.2 us
    add x3, other arithmetic, multiply_by(): coef_real * field_imag + coef_imag * field_real  13.3 us
  transfers between devices with their start and end apart: 11, of which 9 were waited for; matrix products, arithmetic and copies ran while one was open for 1% of the time, Pallas kernels for 0%

profile of v1, /device:TPU:8, one launch (start us, length us, event | category | flops | bytes accessed | tf_op | source)
XLA Modules:
  0.0 589.7 jit_solution(10953714859771514871)
XLA Ops:
  14.9 3.8 multiply_add_fusion.4
  20.2 3.0 collective-permute-start.1
  24.4 2.4 pad_maximum_fusion.34
  26.8 4.1 collective-permute-start.2
  30.9 1.9 collective-permute-start.3
  32.9 3.1 pad_maximum_fusion.25
  36.0 2.7 collective-permute-done.2
  38.7 4.1 collective-permute-done.3
  42.8 13.2 %fusion.7 = f32[1,64,16,8,128]{4,3,2,1,0:T(8,128)} fusion(f32[1,64,18,1,128]{4,3,2,1,0:T(1,128)} %collective-permute-done.3, f32[1,64,1,8,128]{4,3,2,1,0:T(8,128)S(1)} %collective-permute-done, f32[1,64,1,8,128]{4,3,2,1,0:T(8,128)} %copy-done.6, f32[1,64,16,8,64]{4,3,2,1,0:T(8,128)S(1)} %get-tuple-element.19, f32[1,64,16,8,64]{4,3,2,1,0:T(8,128)} %copy-done.1, ...), kind=kLoop, calls=%fused_computation.21 | loop fusion | flops 19922944 | bytes 16384000 | tf_op jit(solution)/shard_map/add | solution.py:104
  56.0 7.1 %multiply_add_fusion.3 = (f32[1,64,16,8,64]{4,3,2,1,0:T(8,128)S(1)}, f32[1,64,16,8,64]{4,3,2,1,0:T(8,128)S(1)}) fusion(f32[1,64,16,8,128]{4,3,2,1,0:T(8,128)} %fusion.7, f32[64,16,8]{2,1,0:T(8,128)} %copy.16, f32[64,16,8]{2,1,0:T(8,128)} %copy.15), kind=kLoop, calls=%fused_computation.43 | loop fusion | flops 3145728 | bytes 8454144 | tf_op jit(solution)/shard_map/add | solution.py:30
  64.6 10.2 %collective-permute-start.5 = (f32[1,64,1,8,128]{4,3,2,1,0:T(8,128)S(1)}, f32[1,64,1,8,128]{4,3,2,1,0:T(8,128)S(1)}, u32[]{:S(2)}, u32[]{:S(2)}) collective-permute-start(f32[1,64,1,8,128]{4,3,2,1,0:T(8,128)S(1)} %get-tuple-element.13), channel_id=1, source_target_pairs={{0,4},{4,8},{8,12},{1,5},{5,9},{9,13},{2,6},{6,10},{10,14},{3,7},{... | collective-permute-start | bytes 786440 | tf_op jit(solution)/shard_map/ppermute | solution.py:15
  75.9 2.4 pad_maximum_fusion.30
  80.3 4.1 collective-permute-start.7
  84.4 3.1 pad_maximum_fusion.26
  87.5 2.7 collective-permute-done.6
  90.2 1.9 collective-permute-done.7
  92.1 13.2 %fusion.2 = f32[1,64,16,8,128]{4,3,2,1,0:T(8,128)} fusion(f32[1,64,18,1,128]{4,3,2,1,0:T(1,128)} %collective-permute-done.7, f32[1,64,1,8,128]{4,3,2,1,0:T(8,128)S(1)} %collective-permute-done.4, f32[1,64,1,8,128]{4,3,2,1,0:T(8,128)} %copy-done.5, f32[1,64,16,8,64]{4,3,2,1,0:T(8,128)S(1)} %get-tuple-element.17, f32[1,64,16,8,64]{4,3,2,1,0:T(8,128)} %copy-done, ...), kind=kLoop, calls=%fused_computation.4 | loop fusion | flops 19922944 | bytes 16384000 | tf_op jit(solution)/shard_map/add | solution.py:104
  105.4 6.9 %multiply_subtract_fusion.1 = (f32[1,64,16,8,64]{4,3,2,1,0:T(8,128)S(1)}, f32[1,64,16,8,64]{4,3,2,1,0:T(8,128)S(1)}, f32[1,64,16,8,64]{4,3,2,1,0:T(8,128)S(1)}) fusion(f32[]{:T(128)} %bitcast.3, f32[]{:T(128)} %bitcast, f32[1,64,16,8,128]{4,3,2,1,0:T(8,128)} %fusion.2, f32[64,16,8]{2,1,0:T(8,128)} %copy.16, f32[64,16,8]{2,1,0:T(8,128)} %copy.15), kind=kLoop, calls=%fused_computation.40 | loop fusion | flops 4718592 | bytes 10551304 | tf_op jit(solution)/shard_map/sub | solution.py:29
  112.3 2.4 multiply_add_fusion.1
  117.0 4.0 pad_maximum_fusion
  121.1 121.8 %reduce-scatter.2.cloned.1.call-done = f32[4,16,8,256]{3,2,1,0:T(8,128)} async-done(((f32[64,16,8,256]{3,2,1,0:T(8,128)}), f32[4,16,8,256]{3,2,1,0:T(8,128)}) %reduce-scatter.2.cloned.1.call-update) | async-done | bytes 524304 | tf_op jit(solution)/shard_map/reduce_scatter | solution.py:111
  242.8 2.2 convolution_bitcast_fusion
  245.1 174.3 %all-reduce.5.cloned.1.call-done = f32[128,256]{1,0:T(8,128)} async-done(((f32[128,256]{1,0:T(8,128)}), f32[128,256]{1,0:T(8,128)}) %all-reduce.5.cloned.1.call-update) | async-done | bytes 131088 | tf_op jit(solution)/shard_map/psum | solution.py:115
  421.3 160.2 %all-reduce.7.cloned.1.call-done = f32[128,256]{1,0:T(8,128)} async-done(((f32[128,256]{1,0:T(8,128)}), f32[128,256]{1,0:T(8,128)}) %all-reduce.7.cloned.1.call-update) | async-done | bytes 131088 | tf_op jit(solution)/shard_map/psum | solution.py:115
  (46 shorter events, 19.8 us)
Async XLA Ops:
  7.2 6.5 %copy-start.2 = (bf16[64,16,8,128]{3,2,1,0:T(8,128)(2,1)S(1)}, bf16[64,16,8,128]{3,2,1,0:T(8,128)(2,1)}, u32[]{:S(2)}) copy-start(bf16[64,16,8,128]{3,2,1,0:T(8,128)(2,1)} %param.6) | copy-start | bytes 6291460
  7.2 235.7 %reduce-scatter.2.cloned.1.call-start = ((), (), s32[]{:S(2)}) async-start(), calls=%async_computation.1 | async-start | bytes 8912896 | tf_op jit(solution)/shard_map/reduce_scatter | solution.py:111
  13.7 1.0 copy-start.3
  13.7 1.2 copy-start.4
  18.7 14.1 %copy-start.1 = (f32[1,64,16,8,64]{4,3,2,1,0:T(8,128)}, f32[1,64,16,8,64]{4,3,2,1,0:T(8,128)S(1)}, u32[]{:S(2)}) copy-start(f32[1,64,16,8,64]{4,3,2,1,0:T(8,128)S(1)} %get-tuple-element.20) | copy-start | bytes 6291460
  18.9 4.4 collective-permute-start
  20.2 4.2 collective-permute-start.1
  24.4 2.4 copy-start.6
  26.8 11.9 %collective-permute-start.2 = (f32[1,64,18,1,128]{4,3,2,1,0:T(1,128)S(1)}, f32[1,64,18,1,128]{4,3,2,1,0:T(1,128)}, u32[]{:S(2)}, u32[]{:S(2)}) collective-permute-start(f32[1,64,18,1,128]{4,3,2,1,0:T(1,128)S(1)} %get-tuple-element.8), channel_id=1, source_target_pairs={{1,0},{2,1},{3,2},{5,4},{6,5},{7,6},{9,8},{10,9},{11,10},{13,12},{... | collective-permute-start | bytes 1769480 | tf_op jit(solution)/shard_map/ppermute | solution.py:18
  30.9 11.9 %collective-permute-start.3 = (f32[1,64,18,1,128]{4,3,2,1,0:T(1,128)S(1)}, f32[1,64,18,1,128]{4,3,2,1,0:T(1,128)}, u32[]{:S(2)}, u32[]{:S(2)}) collective-permute-start(f32[1,64,18,1,128]{4,3,2,1,0:T(1,128)S(1)} %get-tuple-element.9), channel_id=1, source_target_pairs={{0,1},{1,2},{2,3},{4,5},{5,6},{6,7},{8,9},{9,10},{10,11},{12,13},{... | collective-permute-start | bytes 1769480 | tf_op jit(solution)/shard_map/ppermute | solution.py:15
  63.1 21.3 %copy-start = (f32[1,64,16,8,64]{4,3,2,1,0:T(8,128)}, f32[1,64,16,8,64]{4,3,2,1,0:T(8,128)S(1)}, u32[]{:S(2)}) copy-start(f32[1,64,16,8,64]{4,3,2,1,0:T(8,128)S(1)} %get-tuple-element.18) | copy-start | bytes 6291460
  63.3 11.5 %collective-permute-start.4 = (f32[1,64,1,8,128]{4,3,2,1,0:T(8,128)S(1)}, f32[1,64,1,8,128]{4,3,2,1,0:T(8,128)S(1)}, u32[]{:S(2)}, u32[]{:S(2)}) collective-permute-start(f32[1,64,1,8,128]{4,3,2,1,0:T(8,128)S(1)} %get-tuple-element.14), channel_id=1, source_target_pairs={{4,0},{8,4},{12,8},{5,1},{9,5},{13,9},{6,2},{10,6},{14,10},{7,3},{... | collective-permute-start | bytes 786440 | tf_op jit(solution)/shard_map/ppermute | solution.py:18
  64.6 11.3 %collective-permute-start.5 = (f32[1,64,1,8,128]{4,3,2,1,0:T(8,128)S(1)}, f32[1,64,1,8,128]{4,3,2,1,0:T(8,128)S(1)}, u32[]{:S(2)}, u32[]{:S(2)}) collective-permute-start(f32[1,64,1,8,128]{4,3,2,1,0:T(8,128)S(1)} %get-tuple-element.13), channel_id=1, source_target_pairs={{0,4},{4,8},{8,12},{1,5},{5,9},{9,13},{2,6},{6,10},{10,14},{3,7},{... | collective-permute-start | bytes 786440 | tf_op jit(solution)/shard_map/ppermute | solution.py:15
  75.9 2.4 copy-start.5
  78.3 11.9 %collective-permute-start.6 = (f32[1,64,18,1,128]{4,3,2,1,0:T(1,128)S(1)}, f32[1,64,18,1,128]{4,3,2,1,0:T(1,128)}, u32[]{:S(2)}, u32[]{:S(2)}) collective-permute-start(f32[1,64,18,1,128]{4,3,2,1,0:T(1,128)S(1)} %get-tuple-element.6), channel_id=1, source_target_pairs={{1,0},{2,1},{3,2},{5,4},{6,5},{7,6},{9,8},{10,9},{11,10},{13,12},{... | collective-permute-start | bytes 1769480 | tf_op jit(solution)/shard_map/ppermute | solution.py:18
  80.3 11.9 %collective-permute-start.7 = (f32[1,64,18,1,128]{4,3,2,1,0:T(1,128)S(1)}, f32[1,64,18,1,128]{4,3,2,1,0:T(1,128)}, u32[]{:S(2)}, u32[]{:S(2)}) collective-permute-start(f32[1,64,18,1,128]{4,3,2,1,0:T(1,128)S(1)} %get-tuple-element.7), channel_id=1, source_target_pairs={{0,1},{1,2},{2,3},{4,5},{5,6},{6,7},{8,9},{9,10},{10,11},{12,13},{... | collective-permute-start | bytes 1769480 | tf_op jit(solution)/shard_map/ppermute | solution.py:15
  121.0 298.4 %all-reduce.5.cloned.1.call-start = ((), (), s32[]{:S(2)}) async-start(), calls=%async_computation.2 | async-start | bytes 262144 | tf_op jit(solution)/shard_map/psum | solution.py:115
  245.0 336.5 %all-reduce.7.cloned.1.call-start = ((), (), s32[]{:S(2)}) async-start(), calls=%async_computation.3 | async-start | bytes 262144 | tf_op jit(solution)/shard_map/psum | solution.py:115
Sparse Core Ops, SparseCore 0:
  121.1 121.6 reduce-scatter.1
  246.0 173.3 all-reduce.4
  422.2 159.2 all-reduce.6
